TPU v7x, 32 devices: a whole 2x2x4 slice. The times are simulated.
32 devices in a mesh: groups: 2 (over x), tm: 8 (over z, y), space: 2 (over core).
Axes of the slice: x: 2, y: 2, z: 4, core: 2. Of those that a mesh axis runs over, the one named last changes fastest.
Arguments:
- initial: float32 [128, 4096], P(('groups', 'space')), parts along dimension 0, may hold values from -6 to 6
- guess: float32 [16, 64, 4096], P(('groups', 'tm'), 'space'), parts along dimension 0, may hold values from -6 to 6
- source: float32 [16, 64, 4096], P(('groups', 'tm'), 'space'), parts along dimension 0, may hold values from -12 to 12
- kappa: float32 [64, 4096], P('space'), may hold values from 0.25 to 1
- speed_x: float32 [64, 4096], P('space'), may hold values from -0.4 to 0.4
- speed_y: float32 [64, 4096], P('space'), may hold values from -0.4 to 0.4
Outputs:
- corrected: float32 [16, 64, 4096], P(('groups', 'tm'), 'space'), parts along dimension 0
- new_residual: float32 [16, 64, 4096], P(('groups', 'tm'), 'space'), parts along dimension 0
There are 2 independent parts, one for each index of `groups`. A program takes and returns all parts, laid end to end along the dimension named above; an argument that names none is the same for every part. Nothing has to cross between parts.
All inputs are finite; a program needn't handle non-finite values.
Results may differ from a plain program's by a relative error of at most 0.000031.
Values sent between devices are 32-bit elements; how exact they have to be, the bound alone decides.
A program may use at most 64 MiB of HBM per device.

v0:
```python
import jax
import jax.numpy as jnp
from jax import lax
from jax.sharding import PartitionSpec as P

SUB = 8


fine_tau = 0.025


def padded_2(block, sides, width):
    for axis, dim in sides:
        count = lax.axis_size(axis)
        forward = [(i, i + 1) for i in range(count - 1)]
        backward = [(target, source) for source, target in forward]
        low = lax.ppermute(
            lax.slice_in_dim(block, block.shape[dim] - width, None, axis=dim), axis, forward
        )
        high = lax.ppermute(lax.slice_in_dim(block, 0, width, axis=dim), axis, backward)
        block = jnp.concatenate([low, block, high], axis=dim)
    return block


def shifted_2(value, axis, steps):
    count = lax.axis_size(axis)
    initial, last = (max(0, -steps), min(count, count - steps))
    return lax.ppermute(value, axis, [(source, source + steps) for source in range(initial, last)])


def faces_from(padded):
    middle = padded[1:-1]
    sided = jnp.pad(middle, ((0, 0), (1, 1)))
    north = 0.5 * (middle + padded[:-2])
    south = 0.5 * (middle + padded[2:])
    west = 0.5 * (middle + sided[:, :-2])
    east = 0.5 * (middle + sided[:, 2:])
    return (north, south, west, east)


def local_step(field, padded, faces, speed_x, speed_y, tau, drive_src):
    padded = jnp.pad(padded, ((0, 0), (1, 1)))
    up_row = padded[:-2, 1:-1]
    down_row = padded[2:, 1:-1]
    left_col = padded[1:-1, :-2]
    right_col = padded[1:-1, 2:]
    flux = (
        faces[0] * (up_row - field)
        + faces[1] * (down_row - field)
        + faces[2] * (left_col - field)
        + faces[3] * (right_col - field)
    )
    adv = 0.5 * (speed_x * (right_col - left_col) + speed_y * (down_row - up_row))
    drive = flux - adv
    if drive_src is not None:
        drive = drive + drive_src
    return field + tau * drive


def advance(field, faces, speed_x, speed_y, tau, drive_src):
    padded = padded_2(field, (("space", 0),), 1)
    return local_step(field, padded, faces, speed_x, speed_y, tau, drive_src)


def previous_end(values, initial):
    shifted = shifted_2(values, "tm", 1)
    return jnp.where(lax.axis_index("tm") == 0, initial, shifted)


def local(initial, guess, source, kappa, speed_x, speed_y):
    current = guess[0]
    src = source[0]
    padded_k = padded_2(kappa, (("space", 0),), 1)
    faces = faces_from(padded_k)

    def interval(start):
        return lax.fori_loop(
            0, SUB, lambda turn, u: advance(u, faces, speed_x, speed_y, fine_tau, src), start
        )

    def coarse_step(err):
        return advance(err, faces, speed_x, speed_y, SUB * fine_tau, None)

    resid = interval(previous_end(current, initial)) - current

    def relay(turn, err):
        return coarse_step(shifted_2(err, "tm", 1)) + resid

    err = lax.fori_loop(0, lax.axis_size("tm"), relay, jnp.zeros_like(resid))
    corrected = current + err
    new_residual = interval(previous_end(corrected, initial)) - corrected
    return (corrected[None], new_residual[None])


def solution(mesh):
    in_specs = (
        P(("groups", "space"), None),
        P(("groups", "tm"), "space", None),
        P(("groups", "tm"), "space", None),
        P("space", None),
        P("space", None),
        P("space", None),
    )
    out_specs = (P(("groups", "tm"), "space", None), P(("groups", "tm"), "space", None))
    return jax.shard_map(local, mesh=mesh, in_specs=in_specs, out_specs=out_specs, check_vma=False)
```

profile of v0, /device:TPU:25, one launch (start us, length us, event | category | flops | bytes accessed | tf_op | source)
XLA Modules:
  0.0 398.0 jit_solution(13482889884180108909)
XLA Ops:
  2.9 3.0 collective-permute-start.8
  6.0 3.1 collective-permute-start.9
  9.2 2.3 add_multiply_fusion
  11.5 11.1 %collective-permute-done.9 = f32[32,4096]{1,0:T(8,128)S(1)} collective-permute-done((f32[32,4096]{1,0:T(8,128)}, f32[32,4096]{1,0:T(8,128)S(1)}, u32[]{:S(2)}, u32[]{:S(2)}) %collective-permute-start.9) | collective-permute-done | bytes 524320 | tf_op jit(solution)/shard_map/ppermute | solution.py:28
  23.5 72.3 %while.37 = (s32[]{:T(128)}, f32[32,4096]{1,0:T(8,128)}, f32[32,4096]{1,0:T(8,128)S(1)}, f32[32,4096]{1,0:T(8,128)S(1)}, f32[32,4096]{1,0:T(8,128)S(1)}, /*index...) while((s32[]{:T(128)}, f32[32,4096]{1,0:T(8,128)}, ...), condition=%wide.region_1.2_spmd, body=%wide.region_0.1_spmd.sunk | while | flops 4129314 | bytes 10256865 | solution.py:77
  24.5 2.3 collective-permute-start
  30.3 2.5 fusion.63
  33.8 2.1 collective-permute-start
  39.3 2.5 fusion.63
  42.8 2.1 collective-permute-start
  48.3 2.5 fusion.63
  51.8 2.1 collective-permute-start
  57.3 2.5 fusion.63
  60.8 2.1 collective-permute-start
  66.3 2.5 fusion.63
  69.8 2.1 collective-permute-start
  75.3 2.5 fusion.63
  78.8 2.1 collective-permute-start
  84.3 2.5 fusion.63
  87.9 2.1 collective-permute-start
  93.3 2.5 fusion.63
  97.8 206.9 %while.39 = (s32[]{:T(128)}, f32[32,4096]{1,0:T(8,128)}, f32[32,4096]{1,0:T(8,128)S(1)}, f32[32,4096]{1,0:T(8,128)S(1)}, f32[32,4096]{1,0:T(8,128)S(1)}, /*index...) while((s32[]{:T(128)}, f32[32,4096]{1,0:T(8,128)}, ...), condition=%wide.region_3.4_spmd.clone, body=%wide.region_2.3_spmd.clone.sunk | while | flops 4260387 | bytes 12354075 | solution.py:89
  97.9 2.2 collective-permute-start.4
  100.1 13.9 %collective-permute-done.4 = f32[32,4096]{1,0:T(8,128)S(1)} collective-permute-done((f32[32,4096]{1,0:T(8,128)S(1)}, f32[32,4096]{1,0:T(8,128)S(1)}, u32[]{:S(2)}, u32[]{:S(2)}) %collective-permute-start.4) | collective-permute-done | bytes 524320 | tf_op jit(solution)/shard_map/while/body/eval_jaxpr/ppermute | solution.py:28
  114.1 2.9 collective-permute-start.5
  120.4 2.4 fusion.67
  125.8 14.2 %collective-permute-done.4 = f32[32,4096]{1,0:T(8,128)S(1)} collective-permute-done((f32[32,4096]{1,0:T(8,128)S(1)}, f32[32,4096]{1,0:T(8,128)S(1)}, u32[]{:S(2)}, u32[]{:S(2)}) %collective-permute-start.4) | collective-permute-done | bytes 524320 | tf_op jit(solution)/shard_map/while/body/eval_jaxpr/ppermute | solution.py:28
  140.1 2.9 collective-permute-start.5
  146.4 2.4 fusion.67
  151.8 14.2 %collective-permute-done.4 = f32[32,4096]{1,0:T(8,128)S(1)} collective-permute-done((f32[32,4096]{1,0:T(8,128)S(1)}, f32[32,4096]{1,0:T(8,128)S(1)}, u32[]{:S(2)}, u32[]{:S(2)}) %collective-permute-start.4) | collective-permute-done | bytes 524320 | tf_op jit(solution)/shard_map/while/body/eval_jaxpr/ppermute | solution.py:28
  166.1 2.9 collective-permute-start.5
  172.3 2.4 fusion.67
  177.8 14.2 %collective-permute-done.4 = f32[32,4096]{1,0:T(8,128)S(1)} collective-permute-done((f32[32,4096]{1,0:T(8,128)S(1)}, f32[32,4096]{1,0:T(8,128)S(1)}, u32[]{:S(2)}, u32[]{:S(2)}) %collective-permute-start.4) | collective-permute-done | bytes 524320 | tf_op jit(solution)/shard_map/while/body/eval_jaxpr/ppermute | solution.py:28
  192.0 2.9 collective-permute-start.5
  198.3 2.4 fusion.67
  203.8 14.2 %collective-permute-done.4 = f32[32,4096]{1,0:T(8,128)S(1)} collective-permute-done((f32[32,4096]{1,0:T(8,128)S(1)}, f32[32,4096]{1,0:T(8,128)S(1)}, u32[]{:S(2)}, u32[]{:S(2)}) %collective-permute-start.4) | collective-permute-done | bytes 524320 | tf_op jit(solution)/shard_map/while/body/eval_jaxpr/ppermute | solution.py:28
  218.0 2.9 collective-permute-start.5
  224.3 2.4 fusion.67
  229.8 14.2 %collective-permute-done.4 = f32[32,4096]{1,0:T(8,128)S(1)} collective-permute-done((f32[32,4096]{1,0:T(8,128)S(1)}, f32[32,4096]{1,0:T(8,128)S(1)}, u32[]{:S(2)}, u32[]{:S(2)}) %collective-permute-start.4) | collective-permute-done | bytes 524320 | tf_op jit(solution)/shard_map/while/body/eval_jaxpr/ppermute | solution.py:28
  244.0 2.9 collective-permute-start.5
  250.3 2.4 fusion.67
  255.7 14.2 %collective-permute-done.4 = f32[32,4096]{1,0:T(8,128)S(1)} collective-permute-done((f32[32,4096]{1,0:T(8,128)S(1)}, f32[32,4096]{1,0:T(8,128)S(1)}, u32[]{:S(2)}, u32[]{:S(2)}) %collective-permute-start.4) | collective-permute-done | bytes 524320 | tf_op jit(solution)/shard_map/while/body/eval_jaxpr/ppermute | solution.py:28
  270.0 2.9 collective-permute-start.5
  276.3 2.4 fusion.67
  281.7 14.2 %collective-permute-done.4 = f32[32,4096]{1,0:T(8,128)S(1)} collective-permute-done((f32[32,4096]{1,0:T(8,128)S(1)}, f32[32,4096]{1,0:T(8,128)S(1)}, u32[]{:S(2)}, u32[]{:S(2)}) %collective-permute-start.4) | collective-permute-done | bytes 524320 | tf_op jit(solution)/shard_map/while/body/eval_jaxpr/ppermute | solution.py:28
  296.0 2.9 collective-permute-start.5
  302.3 2.4 fusion.67
  308.0 14.2 %collective-permute-done.10 = f32[32,4096]{1,0:T(8,128)S(1)} collective-permute-done((f32[32,4096]{1,0:T(8,128)S(1)}, f32[32,4096]{1,0:T(8,128)S(1)}, u32[]{:S(2)}, u32[]{:S(2)}) %collective-permute-start.10) | collective-permute-done | bytes 524320 | tf_op jit(solution)/shard_map/ppermute | solution.py:28
  323.1 72.9 %while.38 = (s32[]{:T(128)}, f32[32,4096]{1,0:T(8,128)}, f32[32,4096]{1,0:T(8,128)S(1)}, f32[32,4096]{1,0:T(8,128)S(1)}, f32[32,4096]{1,0:T(8,128)S(1)}, /*index...) while((s32[]{:T(128)}, f32[32,4096]{1,0:T(8,128)}, ...), condition=%wide.region_5.6_spmd, body=%wide.region_4.5_spmd.sunk | while | flops 4129314 | bytes 10256865 | solution.py:77
  324.1 2.9 collective-permute-start.2
  330.4 2.5 fusion.65
  333.9 2.1 collective-permute-start.2
  339.4 2.5 fusion.65
  343.0 2.1 collective-permute-start.2
  348.4 2.5 fusion.65
  352.0 2.1 collective-permute-start.2
  357.4 2.5 fusion.65
  361.0 2.1 collective-permute-start.2
  366.5 2.5 fusion.65
  370.0 2.1 collective-permute-start.2
  375.5 2.5 fusion.65
  379.0 2.1 collective-permute-start.2
  384.5 2.5 fusion.65
  393.5 2.5 fusion.65
  (219 shorter events, 132.4 us)
Async XLA Ops:
  1.6 7.5 %collective-permute-start.7 = (f32[1,4096]{1,0:T(1,128)S(1)}, f32[1,4096]{1,0:T(1,128)S(1)}, u32[]{:S(2)}, u32[]{:S(2)}) collective-permute-start(f32[1,4096]{1,0:T(1,128)S(1)} %get-tuple-element.439), channel_id=1, source_target_pairs={{0,1},{2,3},{4,5},{6,7},{8,9},{10,11},{12,13},{14,15},{16,17},{18,... | collective-permute-start | bytes 49160 | tf_op jit(solution)/shard_map/ppermute | solution.py:17
  2.9 6.2 %collective-permute-start.8 = (f32[1,4096]{1,0:T(1,128)S(1)}, f32[1,4096]{1,0:T(1,128)S(1)}, u32[]{:S(2)}, u32[]{:S(2)}) collective-permute-start(f32[1,4096]{1,0:T(1,128)S(1)} %get-tuple-element.438), channel_id=1, source_target_pairs={{1,0},{3,2},{5,4},{7,6},{9,8},{11,10},{13,12},{15,14},{17,16},{19,... | collective-permute-start | bytes 49160 | tf_op jit(solution)/shard_map/ppermute | solution.py:20
  6.0 16.6 %collective-permute-start.9 = (f32[32,4096]{1,0:T(8,128)}, f32[32,4096]{1,0:T(8,128)S(1)}, u32[]{:S(2)}, u32[]{:S(2)}) collective-permute-start(f32[32,4096]{1,0:T(8,128)} %bitcast.8), channel_id=1, source_target_pairs={{0,2},{2,4},{4,6},{6,8},{8,10},{10,12},{12,14},{1,3},{3,5},{5,7},{... | collective-permute-start | bytes 1572872 | tf_op jit(solution)/shard_map/ppermute | solution.py:28
  9.1 13.5 %copy-start.5 = (f32[32,4096]{1,0:T(8,128)S(1)}, f32[32,4096]{1,0:T(8,128)}, u32[]{:S(2)}) copy-start(f32[32,4096]{1,0:T(8,128)} %param.12) | copy-start | bytes 1572868
  11.5 12.0 %copy-start = (f32[32,4096]{1,0:T(8,128)S(1)}, f32[32,4096]{1,0:T(8,128)}, u32[]{:S(2)}) copy-start(f32[32,4096]{1,0:T(8,128)} %param.16) | copy-start | bytes 1572868
  24.5 3.6 collective-permute-start
  26.9 3.1 collective-permute-start.1
  33.8 3.4 collective-permute-start
  35.9 3.1 collective-permute-start.1
  42.8 3.4 collective-permute-start
  44.9 3.1 collective-permute-start.1
  51.8 3.4 collective-permute-start
  53.9 3.1 collective-permute-start.1
  60.8 3.4 collective-permute-start
  62.9 3.1 collective-permute-start.1
  69.8 3.4 collective-permute-start
  71.9 3.1 collective-permute-start.1
  78.8 3.4 collective-permute-start
  80.9 3.1 collective-permute-start.1
  87.9 3.4 collective-permute-start
  89.9 3.1 collective-permute-start.1
  97.9 16.2 %collective-permute-start.4 = (f32[32,4096]{1,0:T(8,128)S(1)}, f32[32,4096]{1,0:T(8,128)S(1)}, u32[]{:S(2)}, u32[]{:S(2)}) collective-permute-start(f32[32,4096]{1,0:T(8,128)S(1)} %broadcast_select_fusion.4), channel_id=1, source_target_pairs={{0,2},{2,4},{4,6},{6,8},{8,10},{10,12},{12,14},{1,3},{3,5},{5,7},{... | collective-permute-start | bytes 1572872 | tf_op jit(solution)/shard_map/while/body/eval_jaxpr/ppermute | solution.py:28
  114.1 4.2 %collective-permute-start.5 = (f32[1,4096]{1,0:T(1,128)S(1)}, f32[1,4096]{1,0:T(1,128)S(1)}, u32[]{:S(2)}, u32[]{:S(2)}) collective-permute-start(f32[1,4096]{1,0:T(1,128)S(1)} %get-tuple-element.615), channel_id=1, source_target_pairs={{1,0},{3,2},{5,4},{7,6},{9,8},{11,10},{13,12},{15,14},{17,16},{19,... | collective-permute-start | bytes 49160 | tf_op jit(solution)/shard_map/while/body/eval_jaxpr/ppermute | solution.py:20
  117.0 3.1 collective-permute-start.6
  123.9 16.2 %collective-permute-start.4 = (f32[32,4096]{1,0:T(8,128)S(1)}, f32[32,4096]{1,0:T(8,128)S(1)}, u32[]{:S(2)}, u32[]{:S(2)}) collective-permute-start(f32[32,4096]{1,0:T(8,128)S(1)} %broadcast_select_fusion.4), channel_id=1, source_target_pairs={{0,2},{2,4},{4,6},{6,8},{8,10},{10,12},{12,14},{1,3},{3,5},{5,7},{... | collective-permute-start | bytes 1572872 | tf_op jit(solution)/shard_map/while/body/eval_jaxpr/ppermute | solution.py:28
  140.1 4.2 %collective-permute-start.5 = (f32[1,4096]{1,0:T(1,128)S(1)}, f32[1,4096]{1,0:T(1,128)S(1)}, u32[]{:S(2)}, u32[]{:S(2)}) collective-permute-start(f32[1,4096]{1,0:T(1,128)S(1)} %get-tuple-element.615), channel_id=1, source_target_pairs={{1,0},{3,2},{5,4},{7,6},{9,8},{11,10},{13,12},{15,14},{17,16},{19,... | collective-permute-start | bytes 49160 | tf_op jit(solution)/shard_map/while/body/eval_jaxpr/ppermute | solution.py:20
  142.9 3.1 collective-permute-start.6
  149.9 16.2 %collective-permute-start.4 = (f32[32,4096]{1,0:T(8,128)S(1)}, f32[32,4096]{1,0:T(8,128)S(1)}, u32[]{:S(2)}, u32[]{:S(2)}) collective-permute-start(f32[32,4096]{1,0:T(8,128)S(1)} %broadcast_select_fusion.4), channel_id=1, source_target_pairs={{0,2},{2,4},{4,6},{6,8},{8,10},{10,12},{12,14},{1,3},{3,5},{5,7},{... | collective-permute-start | bytes 1572872 | tf_op jit(solution)/shard_map/while/body/eval_jaxpr/ppermute | solution.py:28
  166.1 4.2 %collective-permute-start.5 = (f32[1,4096]{1,0:T(1,128)S(1)}, f32[1,4096]{1,0:T(1,128)S(1)}, u32[]{:S(2)}, u32[]{:S(2)}) collective-permute-start(f32[1,4096]{1,0:T(1,128)S(1)} %get-tuple-element.615), channel_id=1, source_target_pairs={{1,0},{3,2},{5,4},{7,6},{9,8},{11,10},{13,12},{15,14},{17,16},{19,... | collective-permute-start | bytes 49160 | tf_op jit(solution)/shard_map/while/body/eval_jaxpr/ppermute | solution.py:20
  168.9 3.1 collective-permute-start.6
  175.9 16.2 %collective-permute-start.4 = (f32[32,4096]{1,0:T(8,128)S(1)}, f32[32,4096]{1,0:T(8,128)S(1)}, u32[]{:S(2)}, u32[]{:S(2)}) collective-permute-start(f32[32,4096]{1,0:T(8,128)S(1)} %broadcast_select_fusion.4), channel_id=1, source_target_pairs={{0,2},{2,4},{4,6},{6,8},{8,10},{10,12},{12,14},{1,3},{3,5},{5,7},{... | collective-permute-start | bytes 1572872 | tf_op jit(solution)/shard_map/while/body/eval_jaxpr/ppermute | solution.py:28
  192.0 4.2 %collective-permute-start.5 = (f32[1,4096]{1,0:T(1,128)S(1)}, f32[1,4096]{1,0:T(1,128)S(1)}, u32[]{:S(2)}, u32[]{:S(2)}) collective-permute-start(f32[1,4096]{1,0:T(1,128)S(1)} %get-tuple-element.615), channel_id=1, source_target_pairs={{1,0},{3,2},{5,4},{7,6},{9,8},{11,10},{13,12},{15,14},{17,16},{19,... | collective-permute-start | bytes 49160 | tf_op jit(solution)/shard_map/while/body/eval_jaxpr/ppermute | solution.py:20
  194.9 3.1 collective-permute-start.6
  201.8 16.2 %collective-permute-start.4 = (f32[32,4096]{1,0:T(8,128)S(1)}, f32[32,4096]{1,0:T(8,128)S(1)}, u32[]{:S(2)}, u32[]{:S(2)}) collective-permute-start(f32[32,4096]{1,0:T(8,128)S(1)} %broadcast_select_fusion.4), channel_id=1, source_target_pairs={{0,2},{2,4},{4,6},{6,8},{8,10},{10,12},{12,14},{1,3},{3,5},{5,7},{... | collective-permute-start | bytes 1572872 | tf_op jit(solution)/shard_map/while/body/eval_jaxpr/ppermute | solution.py:28
  218.0 4.2 %collective-permute-start.5 = (f32[1,4096]{1,0:T(1,128)S(1)}, f32[1,4096]{1,0:T(1,128)S(1)}, u32[]{:S(2)}, u32[]{:S(2)}) collective-permute-start(f32[1,4096]{1,0:T(1,128)S(1)} %get-tuple-element.615), channel_id=1, source_target_pairs={{1,0},{3,2},{5,4},{7,6},{9,8},{11,10},{13,12},{15,14},{17,16},{19,... | collective-permute-start | bytes 49160 | tf_op jit(solution)/shard_map/while/body/eval_jaxpr/ppermute | solution.py:20
  220.9 3.1 collective-permute-start.6
  227.8 16.2 %collective-permute-start.4 = (f32[32,4096]{1,0:T(8,128)S(1)}, f32[32,4096]{1,0:T(8,128)S(1)}, u32[]{:S(2)}, u32[]{:S(2)}) collective-permute-start(f32[32,4096]{1,0:T(8,128)S(1)} %broadcast_select_fusion.4), channel_id=1, source_target_pairs={{0,2},{2,4},{4,6},{6,8},{8,10},{10,12},{12,14},{1,3},{3,5},{5,7},{... | collective-permute-start | bytes 1572872 | tf_op jit(solution)/shard_map/while/body/eval_jaxpr/ppermute | solution.py:28
  244.0 4.2 %collective-permute-start.5 = (f32[1,4096]{1,0:T(1,128)S(1)}, f32[1,4096]{1,0:T(1,128)S(1)}, u32[]{:S(2)}, u32[]{:S(2)}) collective-permute-start(f32[1,4096]{1,0:T(1,128)S(1)} %get-tuple-element.615), channel_id=1, source_target_pairs={{1,0},{3,2},{5,4},{7,6},{9,8},{11,10},{13,12},{15,14},{17,16},{19,... | collective-permute-start | bytes 49160 | tf_op jit(solution)/shard_map/while/body/eval_jaxpr/ppermute | solution.py:20
  246.9 3.1 collective-permute-start.6
  253.8 16.2 %collective-permute-start.4 = (f32[32,4096]{1,0:T(8,128)S(1)}, f32[32,4096]{1,0:T(8,128)S(1)}, u32[]{:S(2)}, u32[]{:S(2)}) collective-permute-start(f32[32,4096]{1,0:T(8,128)S(1)} %broadcast_select_fusion.4), channel_id=1, source_target_pairs={{0,2},{2,4},{4,6},{6,8},{8,10},{10,12},{12,14},{1,3},{3,5},{5,7},{... | collective-permute-start | bytes 1572872 | tf_op jit(solution)/shard_map/while/body/eval_jaxpr/ppermute | solution.py:28
  270.0 4.2 %collective-permute-start.5 = (f32[1,4096]{1,0:T(1,128)S(1)}, f32[1,4096]{1,0:T(1,128)S(1)}, u32[]{:S(2)}, u32[]{:S(2)}) collective-permute-start(f32[1,4096]{1,0:T(1,128)S(1)} %get-tuple-element.615), channel_id=1, source_target_pairs={{1,0},{3,2},{5,4},{7,6},{9,8},{11,10},{13,12},{15,14},{17,16},{19,... | collective-permute-start | bytes 49160 | tf_op jit(solution)/shard_map/while/body/eval_jaxpr/ppermute | solution.py:20
  272.9 3.1 collective-permute-start.6
  279.8 16.2 %collective-permute-start.4 = (f32[32,4096]{1,0:T(8,128)S(1)}, f32[32,4096]{1,0:T(8,128)S(1)}, u32[]{:S(2)}, u32[]{:S(2)}) collective-permute-start(f32[32,4096]{1,0:T(8,128)S(1)} %broadcast_select_fusion.4), channel_id=1, source_target_pairs={{0,2},{2,4},{4,6},{6,8},{8,10},{10,12},{12,14},{1,3},{3,5},{5,7},{... | collective-permute-start | bytes 1572872 | tf_op jit(solution)/shard_map/while/body/eval_jaxpr/ppermute | solution.py:28
  296.0 4.2 %collective-permute-start.5 = (f32[1,4096]{1,0:T(1,128)S(1)}, f32[1,4096]{1,0:T(1,128)S(1)}, u32[]{:S(2)}, u32[]{:S(2)}) collective-permute-start(f32[1,4096]{1,0:T(1,128)S(1)} %get-tuple-element.615), channel_id=1, source_target_pairs={{1,0},{3,2},{5,4},{7,6},{9,8},{11,10},{13,12},{15,14},{17,16},{19,... | collective-permute-start | bytes 49160 | tf_op jit(solution)/shard_map/while/body/eval_jaxpr/ppermute | solution.py:20
  298.9 3.1 collective-permute-start.6
  304.7 17.5 %copy-start.6 = (f32[32,4096]{1,0:T(8,128)S(1)}, f32[32,4096]{1,0:T(8,128)}, u32[]{:S(2)}) copy-start(f32[32,4096]{1,0:T(8,128)} %param.12) | copy-start | bytes 1572868
  306.0 17.0 %copy-start.4 = (f32[32,4096]{1,0:T(8,128)}, f32[32,4096]{1,0:T(8,128)S(1)}, u32[]{:S(2)}) copy-start(f32[32,4096]{1,0:T(8,128)S(1)} %bitcast_add_fusion) | copy-start | bytes 1572868
  306.0 16.2 %collective-permute-start.10 = (f32[32,4096]{1,0:T(8,128)S(1)}, f32[32,4096]{1,0:T(8,128)S(1)}, u32[]{:S(2)}, u32[]{:S(2)}) collective-permute-start(f32[32,4096]{1,0:T(8,128)S(1)} %bitcast_add_fusion), channel_id=1, source_target_pairs={{0,2},{2,4},{4,6},{6,8},{8,10},{10,12},{12,14},{1,3},{3,5},{5,7},{... | collective-permute-start | bytes 1572872 | tf_op jit(solution)/shard_map/ppermute | solution.py:28
  324.1 4.2 %collective-permute-start.2 = (f32[1,4096]{1,0:T(1,128)S(1)}, f32[1,4096]{1,0:T(1,128)S(1)}, u32[]{:S(2)}, u32[]{:S(2)}) collective-permute-start(f32[1,4096]{1,0:T(1,128)S(1)} %get-tuple-element.604), channel_id=1, source_target_pairs={{1,0},{3,2},{5,4},{7,6},{9,8},{11,10},{13,12},{15,14},{17,16},{19,... | collective-permute-start | bytes 49160 | tf_op jit(solution)/shard_map/while/body/eval_jaxpr/ppermute | solution.py:20
  327.0 3.1 collective-permute-start.3
  333.9 3.4 collective-permute-start.2
  336.0 3.1 collective-permute-start.3
  343.0 3.4 collective-permute-start.2
  345.0 3.1 collective-permute-start.3
  352.0 3.4 collective-permute-start.2
  354.0 3.1 collective-permute-start.3
  361.0 3.4 collective-permute-start.2
  363.1 3.1 collective-permute-start.3
  370.0 3.4 collective-permute-start.2
  372.1 3.1 collective-permute-start.3
  379.0 3.4 collective-permute-start.2
  381.1 3.1 collective-permute-start.3
  388.0 3.4 collective-permute-start.2
  390.1 3.1 collective-permute-start.3
  (24 other events, 50.3 us)
where the time goes:
time: 402 us; the launch traced here: 398 us
  waiting for transfers between devices  181 us (45%)
  starting transfers between devices  113 us (28%)
  other arithmetic  83.2 us (21%)
  local copies, waits for them, and re-layouts  18.4 us (5%)
    ppermute x10, waiting for transfers between devices, shifted_2(): lax.ppermute(value, axis, [(source, source + steps) for source in range(i...  139 us
    ppermute x25, starting transfers between devices, padded_2(): lax.ppermute(lax.slice_in_dim(block, 0, width, axis=dim), axis, backward)  60.1 us
    ppermute x25, waiting for transfers between devices, padded_2(): lax.ppermute(lax.slice_in_dim(block, block.shape[dim] - width, None, axis...  42.1 us
    add x16, other arithmetic, local_step(): return field + tau * drive  39.4 us
    ppermute x25, starting transfers between devices, padded_2(): lax.ppermute(lax.slice_in_dim(block, block.shape[dim] - width, None, axis...  32.3 us
    ppermute x10, starting transfers between devices, shifted_2(): lax.ppermute(value, axis, [(source, source + steps) for source in range(i...  20.8 us
    add x8, other arithmetic, relay(): return coarse_step(shifted_2(err, 'tm', 1)) + resid  19.4 us
    while x64, local copies, waits for them, and re-layouts  16.8 us
  transfers between devices with their start and end apart: 60, of which 34 were waited for; matrix products, arithmetic and copies ran while one was open for 1% of the time, Pallas kernels for 0%

commit v1 on v0

v1 whole, which is shorter than its diff:
```python
import functools
import jax
import jax.numpy as jnp
from jax import lax
from jax.experimental import pallas as pl
from jax.experimental.pallas import tpu as pltpu
from jax.sharding import PartitionSpec as P

SUB = 8
FINE_TAU = 0.025
MESH = pl.DeviceIdType.MESH
HALO = 8
PAD = 256
SWEEP = 512
CHUNK = 256


def kernel(
    count,
    init_ref, guess_ref, src_ref, kap_ref, sx_ref, sy_ref,
    cor_ref, res_ref,
    st, kb, xb, yb, ts, ua, ub, an, as_, aw, ae, c0, dd, rr, ex, ee, rs, er, eh,
    sib_send, sib_recv, g_send, g_recv, gh_send, gh_recv, r_send, r_recv, rh_send, rh_recv,
    x_send, x_recv, xh_send, xh_recv, e_send, e_recv, h_send, h_recv,
):
    j = lax.axis_index("tm")
    s = lax.axis_index("space")
    n = guess_ref.shape[1]
    rows = guess_ref.shape[0]
    tall = rows + HALO
    chunks = n // CHUNK
    odd = lax.rem(j, 2) == 1
    even = lax.rem(j, 2) == 0
    own = pl.multiple_of(HALO * s, HALO)
    hal = pl.multiple_of(rows * (1 - s), HALO)
    bnd = pl.multiple_of((rows - HALO) * (1 - s), HALO)
    edge = pl.multiple_of((rows - HALO) * (1 - s) + HALO * s, HALO)
    there = pl.multiple_of(rows * s, HALO)

    def dev(step):
        return {"tm": lax.rem(j + step + count, count)}

    sibling = {"space": 1 - s}

    barrier = pltpu.get_barrier_semaphore()
    greeted = 1
    pl.semaphore_signal(barrier, inc=1, device_id=sibling, device_id_type=MESH)
    for step in (-2, -1, 1, 2):
        there_is = jnp.logical_and(j + step >= 0, j + step < count)

        @pl.when(there_is)
        def _(step=step):
            pl.semaphore_signal(barrier, inc=1, device_id=dev(step), device_id_type=MESH)

        greeted = greeted + there_is.astype(jnp.int32)
    pl.semaphore_wait(barrier, greeted)

    def remote(src, dst, send, recv, device):
        return pltpu.make_async_remote_copy(
            src_ref=src, dst_ref=dst, send_sem=send, recv_sem=recv,
            device_id=device, device_id_type=MESH,
        )

    def cols(c, pad):
        return pl.ds(pl.multiple_of(pad + c * CHUNK, 128), CHUNK)

    def ownr():
        return pl.ds(own, rows)

    def guess_copy(c):
        return remote(guess_ref.at[:, cols(c, 0)], st.at[ownr(), cols(c, PAD)],
                      g_send.at[c], g_recv.at[c], dev(1))

    def forward(buf, send, recv, c):
        return remote(buf.at[pl.ds(edge, HALO), cols(c, PAD)],
                      buf.at[pl.ds(there, HALO), cols(c, PAD)],
                      send.at[c], recv.at[c], sibling)

    def landed(buf, send, recv, c):
        return remote(buf.at[pl.ds(edge, HALO), cols(c, PAD)],
                      buf.at[pl.ds(hal, HALO), cols(c, PAD)],
                      send.at[c], recv.at[c], sibling)

    def r_copy(c):
        return remote(rs.at[:, cols(c, PAD)], rr.at[ownr(), cols(c, PAD)],
                      r_send.at[c], r_recv.at[c], dev(1))

    def x_copy(c):
        return remote(er.at[:, cols(c, 0)], ex.at[ownr(), cols(c, PAD)],
                      x_send.at[c], x_recv.at[c], dev(2))

    def e_copy(c):
        return remote(ex.at[ownr(), cols(c, PAD)], ee.at[ownr(), cols(c, PAD)],
                      e_send.at[c], e_recv.at[c], dev(-1))

    def h_copy(c):
        return remote(ee.at[pl.ds(edge, HALO), cols(c, PAD)], eh.at[:, cols(c, 0)],
                      h_send.at[c], h_recv.at[c], sibling)

    has_next = j < count - 1

    @pl.when(has_next)
    def _():
        @pl.loop(0, chunks)
        def _(c):
            guess_copy(c).start()

    given = ((kap_ref, kb), (sx_ref, xb), (sy_ref, yb), (src_ref, ts))

    def sib_copy(at, send_side):
        a, b = given[at]
        return remote(a.at[pl.ds(bnd, HALO), :],
                      b.at[pl.ds(there if send_side else hal, HALO), pl.ds(PAD, n)],
                      sib_send.at[at], sib_recv.at[at], sibling)

    for at in range(4):
        sib_copy(at, True).start()
    for buf in (st, kb, ua, ub, an, as_, aw, ae, dd, rr, ex, ee):
        buf[:, :PAD] = jnp.zeros((tall, PAD), jnp.float32)
        buf[:, PAD + n:] = jnp.zeros((tall, PAD), jnp.float32)
    for a, b in given:
        b[ownr(), PAD:PAD + n] = a[...]

    @pl.when(j == 0)
    def _():
        st[ownr(), PAD:PAD + n] = init_ref[...]
        ee[:, PAD:PAD + n] = jnp.zeros((tall, n), jnp.float32)

        @pl.loop(0, chunks)
        def _(c):
            forward(st, gh_send, gh_recv, c).start()

    @pl.when(j == 1)
    def _():
        ex[:, PAD:PAD + n] = jnp.zeros((tall, n), jnp.float32)

    for at in range(4):
        sib_copy(at, False).wait_recv()

    def wide(buf, lo, width):
        return buf[:, pl.ds(pl.multiple_of(lo - 128, 128), width + 256)]

    def sides(block, width):
        left = pltpu.roll(block, 1, 1)[:, 128:128 + width]
        right = pltpu.roll(block, width + 255, 1)[:, 128:128 + width]
        middle = block[:, 128:128 + width]
        return middle, pltpu.roll(middle, 1, 0), pltpu.roll(middle, tall - 1, 0), left, right

    @pl.loop(0, n // SWEEP)
    def _(c):
        lo = pl.multiple_of(PAD + c * SWEEP, 128)
        at = pl.ds(lo, SWEEP)
        k, kn, ks, kw, ke = sides(wide(kb, lo, SWEEP), SWEEP)
        line = lax.broadcasted_iota(jnp.int32, (tall, SWEEP), 0)
        first, last = line == 0, line == tall - 1
        cn = 0.5 * (k + jnp.where(first, 0.0, kn))
        cs = 0.5 * (k + jnp.where(last, 0.0, ks))
        cw = 0.5 * (k + kw)
        ce = 0.5 * (k + ke)
        sx, sy = 0.5 * xb[:, at], 0.5 * yb[:, at]
        an[:, at] = jnp.where(first, 0.0, FINE_TAU * (cn + sy))
        as_[:, at] = jnp.where(last, 0.0, FINE_TAU * (cs - sy))
        aw[:, at] = FINE_TAU * (cw + sx)
        ae[:, at] = FINE_TAU * (ce - sx)
        total = FINE_TAU * ((cn + cs) + (cw + ce))
        dd[:, at] = total
        c0[:, at] = 1.0 - total
        ts[:, at] = FINE_TAU * ts[:, at]

    def sweep(a, b):
        @pl.loop(0, n // SWEEP)
        def _(c):
            lo = pl.multiple_of(PAD + c * SWEEP, 128)
            at = pl.ds(lo, SWEEP)
            u, un, us, uw, ue = sides(wide(a, lo, SWEEP), SWEEP)
            b[:, at] = ((c0[:, at] * u + ts[:, at]) + (an[:, at] * un + as_[:, at] * us)
                        + (aw[:, at] * uw + ae[:, at] * ue))

    def interval(a):
        sweep(a, ub)

        @pl.loop(0, (SUB - 2) // 2)
        def _(_turn):
            sweep(ub, ua)
            sweep(ua, ub)

        sweep(ub, ua)

    def coarse(buf, lo):
        at = pl.ds(lo, CHUNK)
        u, un, us, uw, ue = sides(wide(buf, lo, CHUNK), CHUNK)
        drive = ((an[:, at] * un + as_[:, at] * us) + (aw[:, at] * uw + ae[:, at] * ue)
                 - dd[:, at] * u)
        return u + float(SUB) * drive

    @pl.when(j > 0)
    def _():
        @pl.loop(0, chunks)
        def _(c):
            guess_copy(c).wait_recv()
            forward(st, gh_send, gh_recv, c).start()

    @pl.loop(0, chunks)
    def _(c):
        landed(st, gh_send, gh_recv, c).wait_recv()

    interval(st)

    @pl.loop(0, chunks)
    def _(c):
        at = cols(c, PAD)
        rs[:, at] = ua[ownr(), at] - guess_ref[:, cols(c, 0)]

        @pl.when(even)
        def _():
            r_copy(c).start()

    def finish(c):
        at = cols(c, PAD)
        lo = pl.multiple_of(PAD + c * CHUNK, 128)
        ua[:, at] = coarse(ee, lo)
        err = ua[ownr(), at] + rs[:, at]
        cor_ref[:, cols(c, 0)] = guess_ref[:, cols(c, 0)] + err
        return err

    sends_x = jnp.logical_and(odd, j + 2 < count)
    takes_x = jnp.logical_and(odd, j > 1)
    takes_e = jnp.logical_and(even, j > 0)

    @pl.when(odd)
    def _():
        @pl.loop(0, chunks + 1)
        def _(c):
            @pl.when(c < chunks)
            def _():
                r_copy(c).wait_recv()
                forward(rr, rh_send, rh_recv, c).start()

                @pl.when(takes_x)
                def _():
                    x_copy(c).wait_recv()
                    forward(ex, xh_send, xh_recv, c).start()
                    e_copy(c).start()

                landed(rr, rh_send, rh_recv, c).wait_recv()

                @pl.when(takes_x)
                def _():
                    landed(ex, xh_send, xh_recv, c).wait_recv()

            lo = pl.multiple_of(PAD - 128 + c * CHUNK, 128)
            at = pl.ds(lo, CHUNK)
            ee[:, at] = coarse(ex, lo) + rr[:, at]

            @pl.when(c > 0)
            def _():
                h_copy(c - 1).start()
                er[:, cols(c - 1, 0)] = finish(c - 1)

                @pl.when(sends_x)
                def _():
                    x_copy(c - 1).start()

        @pl.loop(0, chunks)
        def _(c):
            h_copy(c).wait_recv()
            at = cols(c, PAD)
            ua[:, at] = st[:, at] + ee[:, at]
            ua[pl.ds(hal, HALO), at] = st[pl.ds(hal, HALO), at] + eh[:, cols(c, 0)]

    @pl.when(even)
    def _():
        @pl.loop(0, chunks + 1)
        def _(c):
            @pl.when(jnp.logical_and(c < chunks, takes_e))
            def _():
                e_copy(c).wait_recv()
                forward(ee, xh_send, xh_recv, c).start()
                landed(ee, xh_send, xh_recv, c).wait_recv()

            @pl.when(c > 0)
            def _():
                finish(c - 1)

        @pl.loop(0, chunks)
        def _(c):
            at = cols(c, PAD)
            ua[:, at] = st[:, at] + ee[:, at]

    interval(ua)

    @pl.loop(0, chunks)
    def _(c):
        at = cols(c, 0)
        res_ref[:, at] = ua[ownr(), cols(c, PAD)] - cor_ref[:, at]

    for at in range(4):
        sib_copy(at, True).wait_send()

    @pl.loop(0, chunks)
    def _(c):
        forward(st, gh_send, gh_recv, c).wait_send()

        @pl.when(has_next)
        def _():
            guess_copy(c).wait_send()

        @pl.when(even)
        def _():
            r_copy(c).wait_send()

        @pl.when(odd)
        def _():
            forward(rr, rh_send, rh_recv, c).wait_send()
            h_copy(c).wait_send()

        @pl.when(takes_x)
        def _():
            forward(ex, xh_send, xh_recv, c).wait_send()
            e_copy(c).wait_send()

        @pl.when(sends_x)
        def _():
            x_copy(c).wait_send()

        @pl.when(takes_e)
        def _():
            forward(ee, xh_send, xh_recv, c).wait_send()


def local(initial, guess, source, kappa, speed_x, speed_y):
    count = lax.axis_size("tm")
    rows, n = kappa.shape
    chunks = n // CHUNK
    tall = rows + HALO
    big = pltpu.VMEM((tall, n + 2 * PAD), jnp.float32)
    sems = pltpu.SemaphoreType.DMA
    cor, res = pl.pallas_call(
        functools.partial(kernel, count),
        out_shape=[jax.ShapeDtypeStruct((rows, n), jnp.float32)] * 2,
        in_specs=[pl.BlockSpec(memory_space=pltpu.VMEM)] * 6,
        out_specs=[pl.BlockSpec(memory_space=pltpu.VMEM)] * 2,
        scratch_shapes=[big] * 16 + [
            pltpu.VMEM((rows, n + 2 * PAD), jnp.float32),
            pltpu.VMEM((rows, n), jnp.float32),
            pltpu.VMEM((HALO, n), jnp.float32),
        ] + [sems((4,))] * 2 + [sems((chunks,))] * 16,
        compiler_params=pltpu.CompilerParams(
            collective_id=0, has_side_effects=True, vmem_limit_bytes=40 * 1024 * 1024
        ),
    )(initial, guess[0], source[0], kappa, speed_x, speed_y)
    return cor[None], res[None]


def solution(mesh):
    in_specs = (
        P(("groups", "space"), None),
        P(("groups", "tm"), "space", None),
        P(("groups", "tm"), "space", None),
        P("space", None),
        P("space", None),
        P("space", None),
    )
    out_specs = (P(("groups", "tm"), "space", None), P(("groups", "tm"), "space", None))
    return jax.shard_map(local, mesh=mesh, in_specs=in_specs, out_specs=out_specs, check_vma=False)
```

time: 402 us -> 79.9 us (0.20)
  waiting for transfers between devices: 181 us -> 0 us
  starting transfers between devices: 113 us -> 0 us
  other arithmetic: 83.2 us -> 0 us
  Pallas kernels: 0 us -> 71 us
  local copies, waits for them, and re-layouts: 18.4 us -> 7.83 us
    ppermute x60 -> x0, waiting for transfers between devices: 181 us -> none  [the longest x10 139 us: shifted_2(): lax.ppermute(value, axis, [(source, source + steps) for source in range(i...]
    ppermute x60 -> x0, starting transfers between devices: 113 us -> none  [the longest x25 60.1 us: padded_2(): lax.ppermute(lax.slice_in_dim(block, 0, width, axis=dim), axis, backward)]
    pallas_call x0 -> x1, Pallas kernels: none -> 71 us  [local(): pl.pallas_call(functools.partial(kernel, count), out_shape=[jax.ShapeDtyp...]
    add x25 -> x0, other arithmetic: 60.1 us -> none  [the longest x16 39.4 us: local_step(): return field + tau * drive]
    while x64 -> x0, local copies, waits for them, and re-layouts: 16.8 us -> none
    unnamed x8 -> x14, local copies, waits for them, and re-layouts: 0.02 us -> 7.83 us
    while x8 -> x0, other arithmetic: 7.58 us -> none
    concatenate x24 -> x0, other arithmetic: 7.4 us -> none  [padded_2(): block = jnp.concatenate([low, block, high], axis=dim)]
  transfers between devices with their start and end apart: 60 -> 0, of which waited for: 34 -> 0; matrix products, arithmetic and copies ran while one was open for 1% -> 0% of each run, Pallas kernels for 0% -> 0%
where the time goes in v1:
time: 79.9 us; the launch traced here: 79.5 us
  Pallas kernels  71 us (89%)
  local copies, waits for them, and re-layouts  7.83 us (10%)
    pallas_call x1, Pallas kernels, local(): pl.pallas_call(functools.partial(kernel, count), out_shape=[jax.ShapeDtyp...  71 us
    unnamed x14, local copies, waits for them, and re-layouts  7.83 us

profile of v1, /device:TPU:25, one launch (start us, length us, event | category | flops | bytes accessed | tf_op | source)
XLA Modules:
  0.0 79.5 jit_solution(10491342319063173208)
XLA Ops:
  0.6 0.0 copy-start
  0.6 1.0 %copy-done = f32[32,4096]{1,0:T(8,128)S(1)} copy-done((f32[32,4096]{1,0:T(8,128)S(1)}, f32[32,4096]{1,0:T(8,128)}, u32[]{:S(2)}) %copy-start) | copy-done | bytes 524312
  1.7 0.0 copy-start.1
  1.7 1.0 %copy-done.1 = f32[1,32,4096]{2,1,0:T(8,128)S(1)} copy-done((f32[1,32,4096]{2,1,0:T(8,128)S(1)}, f32[1,32,4096]{2,1,0:T(8,128)}, u32[]{:S(2)}) %copy-start.1) | copy-done | bytes 524312
  2.7 0.0 copy-start.2
  2.7 1.0 %copy-done.2 = f32[1,32,4096]{2,1,0:T(8,128)S(1)} copy-done((f32[1,32,4096]{2,1,0:T(8,128)S(1)}, f32[1,32,4096]{2,1,0:T(8,128)}, u32[]{:S(2)}) %copy-start.2) | copy-done | bytes 524312
  3.8 0.0 copy-start.3
  3.8 1.0 %copy-done.3 = f32[32,4096]{1,0:T(8,128)S(1)} copy-done((f32[32,4096]{1,0:T(8,128)S(1)}, f32[32,4096]{1,0:T(8,128)}, u32[]{:S(2)}) %copy-start.3) | copy-done | bytes 524312
  4.8 0.0 copy-start.4
  4.8 1.0 %copy-done.4 = f32[32,4096]{1,0:T(8,128)S(1)} copy-done((f32[32,4096]{1,0:T(8,128)S(1)}, f32[32,4096]{1,0:T(8,128)}, u32[]{:S(2)}) %copy-start.4) | copy-done | bytes 524312
  5.8 0.0 copy-start.5
  5.8 1.0 %copy-done.5 = f32[32,4096]{1,0:T(8,128)S(1)} copy-done((f32[32,4096]{1,0:T(8,128)S(1)}, f32[32,4096]{1,0:T(8,128)}, u32[]{:S(2)}) %copy-start.5) | copy-done | bytes 524312
  6.9 71.0 %shard_map.77 = (f32[32,4096]{1,0:T(8,128)S(1)}, f32[32,4096]{1,0:T(8,128)S(1)}) custom-call(f32[32,4096]{1,0:T(8,128)S(1)} %copy-done, f32[32,4096]{1,0:T(8,128)S(1)} %bitcast.6, f32[32,4096]{1,0:T(8,128)S(1)} %bitcast.7, f32[32,4096]{1,0:T(8,128)S(1)} %copy-done.3, f32[32,4096]{1,0:T(8,128)S(1)} %copy-done.4, f32[32,4096]{1,0:T(8,128)S(1)} %copy-done.5), custom_call_target="tpu_custom_call" | custom-call | tf_op jit(solution)/shard_map/pallas_call | solution.py:338
  77.9 0.8 %copy.10 = f32[1,32,4096]{2,1,0:T(8,128)} copy(f32[1,32,4096]{2,1,0:T(8,128)S(1)} %bitcast.5) | data formatting | bytes 1048576
  78.7 0.8 copy.11
Async XLA Ops:
  0.6 1.0 %copy-start = (f32[32,4096]{1,0:T(8,128)S(1)}, f32[32,4096]{1,0:T(8,128)}, u32[]{:S(2)}) copy-start(f32[32,4096]{1,0:T(8,128)} %init_ref.1) | copy-start | bytes 1572868
  1.7 1.0 %copy-start.1 = (f32[1,32,4096]{2,1,0:T(8,128)S(1)}, f32[1,32,4096]{2,1,0:T(8,128)}, u32[]{:S(2)}) copy-start(f32[1,32,4096]{2,1,0:T(8,128)} %param.7) | copy-start | bytes 1572868
  2.7 1.0 %copy-start.2 = (f32[1,32,4096]{2,1,0:T(8,128)S(1)}, f32[1,32,4096]{2,1,0:T(8,128)}, u32[]{:S(2)}) copy-start(f32[1,32,4096]{2,1,0:T(8,128)} %param.8) | copy-start | bytes 1572868
  3.8 1.0 %copy-start.3 = (f32[32,4096]{1,0:T(8,128)S(1)}, f32[32,4096]{1,0:T(8,128)}, u32[]{:S(2)}) copy-start(f32[32,4096]{1,0:T(8,128)} %kap_ref.1) | copy-start | bytes 1572868
  4.8 1.0 %copy-start.4 = (f32[32,4096]{1,0:T(8,128)S(1)}, f32[32,4096]{1,0:T(8,128)}, u32[]{:S(2)}) copy-start(f32[32,4096]{1,0:T(8,128)} %sx_ref.1) | copy-start | bytes 1572868
  5.8 1.0 %copy-start.5 = (f32[32,4096]{1,0:T(8,128)S(1)}, f32[32,4096]{1,0:T(8,128)}, u32[]{:S(2)}) copy-start(f32[32,4096]{1,0:T(8,128)} %sy_ref.1) | copy-start | bytes 1572868

commit v2 on v1

v2 whole, which is shorter than its diff:
```python
import functools
import jax
import jax.numpy as jnp
from jax import lax
from jax.experimental import pallas as pl
from jax.experimental.pallas import tpu as pltpu
from jax.sharding import PartitionSpec as P

SUB = 8
FINE_TAU = 0.025
MESH = pl.DeviceIdType.MESH
HALO = 8
PAD = 256
SWEEP = 512
CHUNK = 256
GRAIN = 512
WINDOW = 1024


def kernel(
    count,
    init_ref, guess_ref, src_ref, kap_ref, sx_ref, sy_ref,
    cor_ref, res_ref,
    st, kb, xb, yb, ts, an, as_, aw, ae, c0, dd, rr, ex, ee, rs, eh, er, gv, wa, wb, tmp,
    sib_send, sib_recv, load, g_send, g_recv, gh_send, gh_recv, r_send, r_recv, rh_send, rh_recv,
    x_send, x_recv, xh_send, xh_recv, e_send, e_recv, eh_send, eh_recv, h_send, h_recv,
):
    j = lax.axis_index("tm")
    s = lax.axis_index("space")
    rows, n = guess_ref.shape
    tall = rows + HALO
    chunks = n // CHUNK
    grains = n // GRAIN
    windows = n // WINDOW
    per_window = WINDOW // CHUNK
    span = WINDOW + 256
    odd = lax.rem(j, 2) == 1
    even = lax.rem(j, 2) == 0
    own = pl.multiple_of(HALO * s, HALO)
    hal = pl.multiple_of(rows * (1 - s), HALO)
    bnd = pl.multiple_of((rows - HALO) * (1 - s), HALO)
    edge = pl.multiple_of((rows - HALO) * (1 - s) + HALO * s, HALO)
    there = pl.multiple_of(rows * s, HALO)
    ownr = pl.ds(own, rows)
    halr = pl.ds(hal, HALO)
    has_next = j < count - 1
    sends_x = jnp.logical_and(odd, j + 2 < count)
    takes_x = jnp.logical_and(odd, j > 1)
    takes_e = jnp.logical_and(even, j > 0)

    def dev(step):
        return {"tm": lax.rem(j + step + count, count)}

    def across(step):
        return {"tm": lax.rem(j + step + count, count), "space": 1 - s}

    sibling = {"space": 1 - s}
    given = ((kap_ref, kb), (sx_ref, xb), (sy_ref, yb), (src_ref, ts))

    def load_copy(at):
        a, b = given[at]
        return pltpu.make_async_copy(a, b.at[ownr, pl.ds(PAD, n)], load.at[at])

    for at in range(4):
        load_copy(at).start()
    guess_load = pltpu.make_async_copy(guess_ref, gv, load.at[4])
    guess_load.start()
    init_load = pltpu.make_async_copy(init_ref, st.at[ownr, pl.ds(PAD, n)], load.at[5])

    @pl.when(j == 0)
    def _():
        init_load.start()

    barrier = pltpu.get_barrier_semaphore()
    greeted = 1
    pl.semaphore_signal(barrier, inc=1, device_id=sibling, device_id_type=MESH)
    for step in (-2, -1, 1, 2):
        there_is = jnp.logical_and(j + step >= 0, j + step < count)
        twice = step in (-2, 2)

        @pl.when(there_is)
        def _(step=step, twice=twice):
            pl.semaphore_signal(barrier, inc=1, device_id=dev(step), device_id_type=MESH)
            if twice:
                pl.semaphore_signal(barrier, inc=1, device_id=across(step), device_id_type=MESH)

        greeted = greeted + there_is.astype(jnp.int32) * (2 if twice else 1)
    pl.semaphore_wait(barrier, greeted)

    def remote(src, dst, send, recv, device):
        return pltpu.make_async_remote_copy(
            src_ref=src, dst_ref=dst, send_sem=send, recv_sem=recv,
            device_id=device, device_id_type=MESH,
        )

    def cols(c, pad, width=CHUNK):
        return pl.ds(pl.multiple_of(pad + c * width, 128), width)

    def guess_copy(g):
        return remote(guess_ref.at[:, cols(g, 0, GRAIN)], st.at[ownr, cols(g, PAD, GRAIN)],
                      g_send.at[g], g_recv.at[g], dev(1))

    def init_copy(g):
        return remote(init_ref.at[pl.ds(bnd, HALO), cols(g, 0, GRAIN)],
                      st.at[pl.ds(there, HALO), cols(g, PAD, GRAIN)],
                      gh_send.at[g], gh_recv.at[g], sibling)

    def forward(buf, send, recv, c, width=CHUNK):
        return remote(buf.at[pl.ds(edge, HALO), cols(c, PAD, width)],
                      buf.at[pl.ds(there, HALO), cols(c, PAD, width)],
                      send.at[c], recv.at[c], sibling)

    def landed(buf, send, recv, c, width=CHUNK):
        return remote(buf.at[pl.ds(edge, HALO), cols(c, PAD, width)],
                      buf.at[halr, cols(c, PAD, width)],
                      send.at[c], recv.at[c], sibling)

    def r_copy(c):
        return remote(rs.at[:, cols(c, PAD)], rr.at[ownr, cols(c, PAD)],
                      r_send.at[c], r_recv.at[c], dev(1))

    def x_copy(c):
        return remote(er.at[:, cols(c, 0)], ex.at[ownr, cols(c, PAD)],
                      x_send.at[c], x_recv.at[c], dev(2))

    def xh_copy(c, rows_there):
        return remote(er.at[pl.ds(bnd, HALO), cols(c, 0)],
                      ex.at[pl.ds(rows_there, HALO), cols(c, PAD)],
                      xh_send.at[c], xh_recv.at[c], across(2))

    def e_copy(c):
        return remote(ex.at[ownr, cols(c, PAD)], ee.at[ownr, cols(c, PAD)],
                      e_send.at[c], e_recv.at[c], dev(-1))

    def h_copy(c):
        return remote(ee.at[pl.ds(edge, HALO), cols(c, PAD)], eh.at[:, cols(c, PAD)],
                      h_send.at[c], h_recv.at[c], sibling)

    @pl.when(has_next)
    def _():
        @pl.loop(0, grains)
        def _(g):
            guess_copy(g).start()

    def sib_copy(at, send_side):
        a, b = given[at]
        return remote(a.at[pl.ds(bnd, HALO), :],
                      b.at[pl.ds(there if send_side else hal, HALO), pl.ds(PAD, n)],
                      sib_send.at[at], sib_recv.at[at], sibling)

    for at in range(4):
        sib_copy(at, True).start()
    for buf in (st, kb, an, as_, aw, ae, c0, dd, ts, rr, ex, ee):
        buf[:, :PAD] = jnp.zeros((tall, PAD), jnp.float32)
        buf[:, PAD + n:] = jnp.zeros((tall, PAD), jnp.float32)
    eh[:, :PAD] = jnp.zeros((HALO, PAD), jnp.float32)
    eh[:, PAD + n:] = jnp.zeros((HALO, PAD), jnp.float32)

    @pl.when(j == 0)
    def _():
        ee[:, PAD:PAD + n] = jnp.zeros((tall, n), jnp.float32)

        @pl.loop(0, grains)
        def _(g):
            init_copy(g).start()

    @pl.when(j == 1)
    def _():
        ex[:, PAD:PAD + n] = jnp.zeros((tall, n), jnp.float32)

    for at in range(4):
        load_copy(at).wait()
    for at in range(4):
        sib_copy(at, False).wait_recv()

    def sides(block, width):
        left = pltpu.roll(block, 1, 1)[:, 128:128 + width]
        right = pltpu.roll(block, width + 255, 1)[:, 128:128 + width]
        middle = block[:, 128:128 + width]
        return middle, pltpu.roll(middle, 1, 0), pltpu.roll(middle, tall - 1, 0), left, right

    def wide(buf, lo, width):
        return buf[:, pl.ds(pl.multiple_of(lo - 128, 128), width + 256)]

    @pl.loop(0, n // SWEEP)
    def _(c):
        lo = pl.multiple_of(PAD + c * SWEEP, 128)
        at = pl.ds(lo, SWEEP)
        k, kn, ks, kw, ke = sides(wide(kb, lo, SWEEP), SWEEP)
        line = lax.broadcasted_iota(jnp.int32, (tall, SWEEP), 0)
        first, last = line == 0, line == tall - 1
        cn = 0.5 * (k + jnp.where(first, 0.0, kn))
        cs = 0.5 * (k + jnp.where(last, 0.0, ks))
        cw = 0.5 * (k + kw)
        ce = 0.5 * (k + ke)
        sx, sy = 0.5 * xb[:, at], 0.5 * yb[:, at]
        an[:, at] = jnp.where(first, 0.0, FINE_TAU * (cn + sy))
        as_[:, at] = jnp.where(last, 0.0, FINE_TAU * (cs - sy))
        aw[:, at] = FINE_TAU * (cw + sx)
        ae[:, at] = FINE_TAU * (ce - sx)
        total = FINE_TAU * ((cn + cs) + (cw + ce))
        dd[:, at] = total
        c0[:, at] = 1.0 - total
        ts[:, at] = FINE_TAU * ts[:, at]

    def fine(at):
        def step(a, b):
            u = a[...]
            un, us = pltpu.roll(u, 1, 0), pltpu.roll(u, tall - 1, 0)
            uw, ue = pltpu.roll(u, 1, 1), pltpu.roll(u, span - 1, 1)
            b[...] = ((c0[:, at] * u + ts[:, at]) + (an[:, at] * un + as_[:, at] * us)
                      + (aw[:, at] * uw + ae[:, at] * ue))

        @pl.loop(0, SUB // 2)
        def _(_turn):
            step(wa, wb)
            step(wb, wa)

    def window_at(w):
        return pl.ds(pl.multiple_of(PAD - 128 + w * WINDOW, 128), span)

    def coarse(buf, lo):
        at = pl.ds(lo, CHUNK)
        u, un, us, uw, ue = sides(wide(buf, lo, CHUNK), CHUNK)
        drive = ((an[:, at] * un + as_[:, at] * us) + (aw[:, at] * uw + ae[:, at] * ue)
                 - dd[:, at] * u)
        return u + float(SUB) * drive

    guess_load.wait()

    @pl.when(j == 0)
    def _():
        init_load.wait()

    def first_window(w):
        at = window_at(w)
        wa[...] = st[:, at]
        fine(at)
        rs[:, cols(w, PAD, WINDOW)] = (wa[ownr, 128:128 + WINDOW]
                                       - gv[:, cols(w, 0, WINDOW)])

        @pl.when(even)
        def _():
            @pl.loop(0, per_window)
            def _(i):
                r_copy(w * per_window + i).start()

    @pl.loop(0, grains + 1)
    def _(g):
        @pl.when(g < grains)
        def _():
            @pl.when(j > 0)
            def _():
                guess_copy(g).wait_recv()
                forward(st, gh_send, gh_recv, g, GRAIN).start()

            landed(st, gh_send, gh_recv, g, GRAIN).wait_recv()

        ratio = WINDOW // GRAIN

        @pl.when(jnp.logical_and(lax.rem(g, ratio) == 0, g > 0))
        def _():
            first_window(g // ratio - 1)

    def finish(c):
        at = cols(c, PAD)
        lo = pl.multiple_of(PAD + c * CHUNK, 128)
        tmp[...] = coarse(ee, lo)
        err = tmp[ownr, :] + rs[:, at]
        cor_ref[:, cols(c, 0)] = gv[:, cols(c, 0)] + err
        return err

    def second_window(w, fresh):
        at = window_at(w)
        wa[...] = st[:, at] + ee[:, at]
        if fresh:
            low = w * per_window + jnp.where(w == 0, 0, 1)
            high = jnp.minimum((w + 1) * per_window + 1, chunks)

            @pl.loop(low, high)
            def _(c):
                h_copy(c).wait_recv()

            wa[halr, :] = st[halr, at] + eh[:, at]
        fine(at)
        out = cols(w, 0, WINDOW)
        res_ref[:, out] = wa[ownr, 128:128 + WINDOW] - cor_ref[:, out]

    @pl.when(odd)
    def _():
        @pl.loop(0, chunks + 1)
        def _(c):
            @pl.when(c < chunks)
            def _():
                r_copy(c).wait_recv()
                forward(rr, rh_send, rh_recv, c).start()

                @pl.when(takes_x)
                def _():
                    x_copy(c).wait_recv()
                    e_copy(c).start()
                    xh_copy(c, hal).wait_recv()

                landed(rr, rh_send, rh_recv, c).wait_recv()

            lo = pl.multiple_of(PAD - 128 + c * CHUNK, 128)
            at = pl.ds(lo, CHUNK)
            ee[:, at] = coarse(ex, lo) + rr[:, at]

            @pl.when(c > 0)
            def _():
                er[:, cols(c - 1, 0)] = finish(c - 1)

                @pl.when(sends_x)
                def _():
                    x_copy(c - 1).start()
                    xh_copy(c - 1, there).start()

                h_copy(c - 1).start()

            late = per_window + 2
            ready = jnp.logical_and(c >= late, lax.rem(c + 2 * per_window - late, per_window) == 0)

            @pl.when(jnp.logical_and(ready, jnp.logical_not(sends_x)))
            def _():
                second_window((c - late) // per_window, True)

        @pl.loop(jnp.where(sends_x, 0, windows - 1), windows)
        def _(w):
            second_window(w, True)

    @pl.when(even)
    def _():
        @pl.loop(0, chunks + 1)
        def _(c):
            @pl.when(jnp.logical_and(c < chunks, takes_e))
            def _():
                e_copy(c).wait_recv()
                forward(ee, eh_send, eh_recv, c).start()
                landed(ee, eh_send, eh_recv, c).wait_recv()

            @pl.when(c > 0)
            def _():
                finish(c - 1)

            @pl.when(jnp.logical_and(c > 0, lax.rem(c, per_window) == 0))
            def _():
                second_window(c // per_window - 1, False)

    for at in range(4):
        sib_copy(at, True).wait_send()

    @pl.loop(0, grains)
    def _(g):
        forward(st, gh_send, gh_recv, g, GRAIN).wait_send()

        @pl.when(has_next)
        def _():
            guess_copy(g).wait_send()

    @pl.loop(0, chunks)
    def _(c):
        @pl.when(even)
        def _():
            r_copy(c).wait_send()

        @pl.when(odd)
        def _():
            forward(rr, rh_send, rh_recv, c).wait_send()
            h_copy(c).wait_send()

        @pl.when(takes_x)
        def _():
            e_copy(c).wait_send()

        @pl.when(sends_x)
        def _():
            x_copy(c).wait_send()
            xh_copy(c, there).wait_send()

        @pl.when(takes_e)
        def _():
            forward(ee, eh_send, eh_recv, c).wait_send()


def local(initial, guess, source, kappa, speed_x, speed_y):
    count = lax.axis_size("tm")
    rows, n = kappa.shape
    chunks = n // CHUNK
    tall = rows + HALO
    wide_n = n + 2 * PAD
    sems = pltpu.SemaphoreType.DMA

    def vmem(*shape):
        return pltpu.VMEM(shape, jnp.float32)

    cor, res = pl.pallas_call(
        functools.partial(kernel, count),
        out_shape=[jax.ShapeDtypeStruct((rows, n), jnp.float32)] * 2,
        in_specs=[pl.BlockSpec(memory_space=pltpu.HBM)] * 6,
        out_specs=[pl.BlockSpec(memory_space=pltpu.VMEM)] * 2,
        scratch_shapes=[vmem(tall, wide_n)] * 14 + [
            vmem(rows, wide_n), vmem(HALO, wide_n), vmem(rows, n), vmem(rows, n),
            vmem(tall, WINDOW + 256), vmem(tall, WINDOW + 256), vmem(tall, CHUNK),
        ] + [sems((4,))] * 2 + [sems((6,))] + [sems((n // GRAIN,))] * 4 + [sems((chunks,))] * 14,
        compiler_params=pltpu.CompilerParams(
            collective_id=0, has_side_effects=True, vmem_limit_bytes=62 * 1024 * 1024
        ),
    )(initial, guess[0], source[0], kappa, speed_x, speed_y)
    return cor[None], res[None]


def solution(mesh):
    in_specs = (
        P(("groups", "space"), None),
        P(("groups", "tm"), "space", None),
        P(("groups", "tm"), "space", None),
        P("space", None),
        P("space", None),
        P("space", None),
    )
    out_specs = (P(("groups", "tm"), "space", None), P(("groups", "tm"), "space", None))
    return jax.shard_map(local, mesh=mesh, in_specs=in_specs, out_specs=out_specs, check_vma=False)
```

time: 79.9 us -> 68 us (0.85)
  Pallas kernels: 71 us -> 64.5 us
  local copies, waits for them, and re-layouts: 7.83 us -> 2.72 us
    pallas_call x1, Pallas kernels: 71 us -> 64.5 us  [local(): pl.pallas_call(functools.partial(kernel, count), out_shape=[jax.ShapeDtyp...]
    unnamed x14 -> x4, local copies, waits for them, and re-layouts: 7.83 us -> 2.72 us
where the time goes in v2:
time: 68 us; the launch traced here: 67.9 us
  Pallas kernels  64.5 us (95%)
  local copies, waits for them, and re-layouts  2.72 us (4%)
    pallas_call x1, Pallas kernels, local(): pl.pallas_call(functools.partial(kernel, count), out_shape=[jax.ShapeDtyp...  64.5 us
    unnamed x4, local copies, waits for them, and re-layouts  2.72 us

profile of v2, /device:TPU:25, one launch (start us, length us, event | category | flops | bytes accessed | tf_op | source)
XLA Modules:
  0.0 67.9 jit_solution(6558969332937481558)
XLA Ops:
  0.6 64.5 %shard_map.77 = (f32[32,4096]{1,0:T(8,128)}, f32[32,4096]{1,0:T(8,128)}) custom-call(f32[32,4096]{1,0:T(8,128)} %init_ref.1, f32[32,4096]{1,0:T(8,128)} %bitcast.6, f32[32,4096]{1,0:T(8,128)} %bitcast.7, f32[32,4096]{1,0:T(8,128)} %kap_ref.1, f32[32,4096]{1,0:T(8,128)} %sx_ref.1, f32[32,4096]{1,0:T(8,128)} %sy_ref.1), custom_call_target="tpu_custom_call" | custom-call | tf_op jit(solution)/shard_map/pallas_call | solution.py:397
  65.2 0.0 copy-start
  65.2 1.9 %copy.10 = f32[1,32,4096]{2,1,0:T(8,128)} copy(f32[1,32,4096]{2,1,0:T(8,128)} %bitcast.5) | data formatting | bytes 1048576
  67.1 0.0 copy-done
  67.1 0.8 %copy.11 = f32[1,32,4096]{2,1,0:T(8,128)} copy(f32[1,32,4096]{2,1,0:T(8,128)S(1)} %bitcast.4) | data formatting | bytes 1048576
Async XLA Ops:
  65.2 1.9 %copy-start = (f32[32,4096]{1,0:T(8,128)S(1)}, f32[32,4096]{1,0:T(8,128)}, u32[]{:S(2)}) copy-start(f32[32,4096]{1,0:T(8,128)} %get-tuple-element.5) | copy-start | bytes 1572868

commit v3 on v2

--- a/solution.py
+++ b/solution.py
@@ -153,6 +153,9 @@
     for buf in (st, kb, an, as_, aw, ae, c0, dd, ts, rr, ex, ee):
         buf[:, :PAD] = jnp.zeros((tall, PAD), jnp.float32)
         buf[:, PAD + n:] = jnp.zeros((tall, PAD), jnp.float32)
+    for buf in (wa, wb):
+        buf[:8, :] = jnp.zeros((8, span), jnp.float32)
+        buf[8 + tall:, :] = jnp.zeros((8, span), jnp.float32)
     eh[:, :PAD] = jnp.zeros((HALO, PAD), jnp.float32)
     eh[:, PAD + n:] = jnp.zeros((HALO, PAD), jnp.float32)
 
@@ -205,11 +208,14 @@
 
     def fine(at):
         def step(a, b):
-            u = a[...]
-            un, us = pltpu.roll(u, 1, 0), pltpu.roll(u, tall - 1, 0)
-            uw, ue = pltpu.roll(u, 1, 1), pltpu.roll(u, span - 1, 1)
-            b[...] = ((c0[:, at] * u + ts[:, at]) + (an[:, at] * un + as_[:, at] * us)
-                      + (aw[:, at] * uw + ae[:, at] * ue))
+            for low in range(0, tall, 8):
+                r = slice(low, low + 8)
+                u = a[low + 8:low + 16, :]
+                un, us = a[low + 7:low + 15, :], a[low + 9:low + 17, :]
+                uw, ue = pltpu.roll(u, 1, 1), pltpu.roll(u, span - 1, 1)
+                b[low + 8:low + 16, :] = (
+                    (c0[r, at] * u + ts[r, at]) + (an[r, at] * un + as_[r, at] * us)
+                    + (aw[r, at] * uw + ae[r, at] * ue))
 
         @pl.loop(0, SUB // 2)
         def _(_turn):
@@ -234,9 +240,9 @@
 
     def first_window(w):
         at = window_at(w)
-        wa[...] = st[:, at]
+        wa[8:8 + tall, :] = st[:, at]
         fine(at)
-        rs[:, cols(w, PAD, WINDOW)] = (wa[ownr, 128:128 + WINDOW]
+        rs[:, cols(w, PAD, WINDOW)] = (wa[pl.ds(own + 8, rows), 128:128 + WINDOW]
                                        - gv[:, cols(w, 0, WINDOW)])
 
         @pl.when(even)
@@ -245,20 +251,22 @@
             def _(i):
                 r_copy(w * per_window + i).start()
 
-    @pl.loop(0, grains + 1)
-    def _(g):
-        @pl.when(g < grains)
-        def _():
-            @pl.when(j > 0)
-            def _():
-                guess_copy(g).wait_recv()
-                forward(st, gh_send, gh_recv, g, GRAIN).start()
-
+    @pl.loop(0, grains + 2)
+    def _(i):
+        @pl.when(jnp.logical_and(i < grains, j > 0))
+        def _():
+            guess_copy(i).wait_recv()
+            forward(st, gh_send, gh_recv, i, GRAIN).start()
+
+        g = i - 1
+
+        @pl.when(jnp.logical_and(g >= 0, g < grains))
+        def _():
             landed(st, gh_send, gh_recv, g, GRAIN).wait_recv()
 
         ratio = WINDOW // GRAIN
 
-        @pl.when(jnp.logical_and(lax.rem(g, ratio) == 0, g > 0))
+        @pl.when(jnp.logical_and(lax.rem(g + ratio, ratio) == 0, g > 0))
         def _():
             first_window(g // ratio - 1)
 
@@ -272,7 +280,7 @@
 
     def second_window(w, fresh):
         at = window_at(w)
-        wa[...] = st[:, at] + ee[:, at]
+        wa[8:8 + tall, :] = st[:, at] + ee[:, at]
         if fresh:
             low = w * per_window + jnp.where(w == 0, 0, 1)
             high = jnp.minimum((w + 1) * per_window + 1, chunks)
@@ -281,20 +289,24 @@
             def _(c):
                 h_copy(c).wait_recv()
 
-            wa[halr, :] = st[halr, at] + eh[:, at]
+            wa[pl.ds(hal + 8, HALO), :] = st[halr, at] + eh[:, at]
         fine(at)
         out = cols(w, 0, WINDOW)
-        res_ref[:, out] = wa[ownr, 128:128 + WINDOW] - cor_ref[:, out]
+        res_ref[:, out] = wa[pl.ds(own + 8, rows), 128:128 + WINDOW] - cor_ref[:, out]
 
     @pl.when(odd)
     def _():
-        @pl.loop(0, chunks + 1)
-        def _(c):
-            @pl.when(c < chunks)
-            def _():
-                r_copy(c).wait_recv()
-                forward(rr, rh_send, rh_recv, c).start()
-
+        @pl.loop(0, chunks + 2)
+        def _(i):
+            @pl.when(i < chunks)
+            def _():
+                r_copy(i).wait_recv()
+                forward(rr, rh_send, rh_recv, i).start()
+
+            c = i - 1
+
+            @pl.when(jnp.logical_and(c >= 0, c < chunks))
+            def _():
                 @pl.when(takes_x)
                 def _():
                     x_copy(c).wait_recv()
@@ -303,9 +315,11 @@
 
                 landed(rr, rh_send, rh_recv, c).wait_recv()
 
-            lo = pl.multiple_of(PAD - 128 + c * CHUNK, 128)
-            at = pl.ds(lo, CHUNK)
-            ee[:, at] = coarse(ex, lo) + rr[:, at]
+            @pl.when(c >= 0)
+            def _():
+                lo = pl.multiple_of(PAD - 128 + c * CHUNK, 128)
+                at = pl.ds(lo, CHUNK)
+                ee[:, at] = coarse(ex, lo) + rr[:, at]
 
             @pl.when(c > 0)
             def _():
@@ -331,19 +345,24 @@
 
     @pl.when(even)
     def _():
-        @pl.loop(0, chunks + 1)
-        def _(c):
-            @pl.when(jnp.logical_and(c < chunks, takes_e))
-            def _():
-                e_copy(c).wait_recv()
-                forward(ee, eh_send, eh_recv, c).start()
+        @pl.loop(0, chunks + 2)
+        def _(i):
+            @pl.when(jnp.logical_and(i < chunks, takes_e))
+            def _():
+                e_copy(i).wait_recv()
+                forward(ee, eh_send, eh_recv, i).start()
+
+            c = i - 1
+
+            @pl.when(jnp.logical_and(jnp.logical_and(c >= 0, c < chunks), takes_e))
+            def _():
                 landed(ee, eh_send, eh_recv, c).wait_recv()
 
             @pl.when(c > 0)
             def _():
                 finish(c - 1)
 
-            @pl.when(jnp.logical_and(c > 0, lax.rem(c, per_window) == 0))
+            @pl.when(jnp.logical_and(c > 0, lax.rem(c + per_window, per_window) == 0))
             def _():
                 second_window(c // per_window - 1, False)
 
@@ -401,7 +420,7 @@
         out_specs=[pl.BlockSpec(memory_space=pltpu.VMEM)] * 2,
         scratch_shapes=[vmem(tall, wide_n)] * 14 + [
             vmem(rows, wide_n), vmem(HALO, wide_n), vmem(rows, n), vmem(rows, n),
-            vmem(tall, WINDOW + 256), vmem(tall, WINDOW + 256), vmem(tall, CHUNK),
+            vmem(tall + 16, WINDOW + 256), vmem(tall + 16, WINDOW + 256), vmem(tall, CHUNK),
         ] + [sems((4,))] * 2 + [sems((6,))] + [sems((n // GRAIN,))] * 4 + [sems((chunks,))] * 14,
         compiler_params=pltpu.CompilerParams(
             collective_id=0, has_side_effects=True, vmem_limit_bytes=62 * 1024 * 1024

time: 68 us -> 57.9 us (0.85)
  Pallas kernels: 64.5 us -> 54.4 us
    pallas_call x1, Pallas kernels: 64.5 us -> 54.4 us  [local(): pl.pallas_call(functools.partial(kernel, count), out_shape=[jax.ShapeDtyp...]
where the time goes in v3:
time: 57.9 us; the launch traced here: 57.8 us
  Pallas kernels  54.4 us (94%)
  local copies, waits for them, and re-layouts  2.72 us (5%)
  between operations  0.65 us (1%)
    pallas_call x1, Pallas kernels, local(): pl.pallas_call(functools.partial(kernel, count), out_shape=[jax.ShapeDtyp...  54.4 us
    unnamed x4, local copies, waits for them, and re-layouts  2.72 us

profile of v3, /device:TPU:25, one launch (start us, length us, event | category | flops | bytes accessed | tf_op | source)
XLA Modules:
  0.0 57.8 jit_solution(16001298454796085889)
XLA Ops:
  0.6 54.4 %shard_map.77 = (f32[32,4096]{1,0:T(8,128)}, f32[32,4096]{1,0:T(8,128)}) custom-call(f32[32,4096]{1,0:T(8,128)} %init_ref.1, f32[32,4096]{1,0:T(8,128)} %bitcast.6, f32[32,4096]{1,0:T(8,128)} %bitcast.7, f32[32,4096]{1,0:T(8,128)} %kap_ref.1, f32[32,4096]{1,0:T(8,128)} %sx_ref.1, f32[32,4096]{1,0:T(8,128)} %sy_ref.1), custom_call_target="tpu_custom_call" | custom-call | tf_op jit(solution)/shard_map/pallas_call | solution.py:416
  55.0 0.0 copy-start
  55.1 1.9 %copy.10 = f32[1,32,4096]{2,1,0:T(8,128)} copy(f32[1,32,4096]{2,1,0:T(8,128)} %bitcast.5) | data formatting | bytes 1048576
  57.0 0.0 copy-done
  57.0 0.8 %copy.11 = f32[1,32,4096]{2,1,0:T(8,128)} copy(f32[1,32,4096]{2,1,0:T(8,128)S(1)} %bitcast.4) | data formatting | bytes 1048576
Async XLA Ops:
  55.0 1.9 %copy-start = (f32[32,4096]{1,0:T(8,128)S(1)}, f32[32,4096]{1,0:T(8,128)}, u32[]{:S(2)}) copy-start(f32[32,4096]{1,0:T(8,128)} %get-tuple-element.5) | copy-start | bytes 1572868

commit v4 on v3

--- a/solution.py
+++ b/solution.py
@@ -334,12 +334,13 @@
 
             late = per_window + 2
             ready = jnp.logical_and(c >= late, lax.rem(c + 2 * per_window - late, per_window) == 0)
+            ready = jnp.logical_and(ready, c < late + (windows - 2) * per_window)
 
             @pl.when(jnp.logical_and(ready, jnp.logical_not(sends_x)))
             def _():
                 second_window((c - late) // per_window, True)
 
-        @pl.loop(jnp.where(sends_x, 0, windows - 1), windows)
+        @pl.loop(jnp.where(sends_x, 0, windows - 2), windows)
         def _(w):
             second_window(w, True)
 

time: 57.9 us -> 57.3 us (0.990)
  Pallas kernels: 54.4 us -> 53.8 us
    pallas_call x1, Pallas kernels: 54.4 us -> 53.8 us  [local(): pl.pallas_call(functools.partial(kernel, count), out_shape=[jax.ShapeDtyp...]
where the time goes in v4:
time: 57.3 us; the launch traced here: 57.2 us
  Pallas kernels  53.8 us (94%)
  local copies, waits for them, and re-layouts  2.72 us (5%)
  between operations  0.65 us (1%)
    pallas_call x1, Pallas kernels, local(): pl.pallas_call(functools.partial(kernel, count), out_shape=[jax.ShapeDtyp...  53.8 us
    unnamed x4, local copies, waits for them, and re-layouts  2.72 us

profile of v4, /device:TPU:25, one launch (start us, length us, event | category | flops | bytes accessed | tf_op | source)
XLA Modules:
  0.0 57.2 jit_solution(11704655881630708110)
XLA Ops:
  0.6 53.8 %shard_map.77 = (f32[32,4096]{1,0:T(8,128)}, f32[32,4096]{1,0:T(8,128)}) custom-call(f32[32,4096]{1,0:T(8,128)} %init_ref.1, f32[32,4096]{1,0:T(8,128)} %bitcast.6, f32[32,4096]{1,0:T(8,128)} %bitcast.7, f32[32,4096]{1,0:T(8,128)} %kap_ref.1, f32[32,4096]{1,0:T(8,128)} %sx_ref.1, f32[32,4096]{1,0:T(8,128)} %sy_ref.1), custom_call_target="tpu_custom_call" | custom-call | tf_op jit(solution)/shard_map/pallas_call | solution.py:417
  54.4 0.0 copy-start
  54.5 1.9 %copy.10 = f32[1,32,4096]{2,1,0:T(8,128)} copy(f32[1,32,4096]{2,1,0:T(8,128)} %bitcast.5) | data formatting | bytes 1048576
  56.4 0.0 copy-done
  56.4 0.8 %copy.11 = f32[1,32,4096]{2,1,0:T(8,128)} copy(f32[1,32,4096]{2,1,0:T(8,128)S(1)} %bitcast.4) | data formatting | bytes 1048576
Async XLA Ops:
  54.4 1.9 %copy-start = (f32[32,4096]{1,0:T(8,128)S(1)}, f32[32,4096]{1,0:T(8,128)}, u32[]{:S(2)}) copy-start(f32[32,4096]{1,0:T(8,128)} %get-tuple-element.5) | copy-start | bytes 1572868
